TPU v7x, 32 devices: a whole 2x2x4 slice. The times are simulated.
32 devices in a mesh: grp: 2 (over x), rows: 8 (over z, y), cols: 2 (over core).
Axes of the slice: x: 2, y: 2, z: 4, core: 2. Of those that a mesh axis runs over, the one named last changes fastest.
Arguments:
- crop_feature_grid: bfloat16 [128, 256, 512], P(('grp', 'rows'), 'cols'), parts along dimension 0, may hold values from -6 to 6
- pixel_layernorm_gain: float32 [512], replicated, may hold values from 0.25 to 1.75
- triple_projection_matrix: bfloat16 [512, 1536], replicated, may hold values from -0.25 to 0.25
- halo_exit_matrix: bfloat16 [512, 512], replicated, may hold values from -0.25 to 0.25
- memory_slots: bfloat16 [256, 512], replicated, may hold values from -6 to 6
- memory_layernorm_gain: float32 [512], replicated, may hold values from 0.25 to 1.75
- memory_asking_matrix: bfloat16 [512, 512], replicated, may hold values from -0.25 to 0.25
- memory_exit_matrix: bfloat16 [512, 512], replicated, may hold values from -0.25 to 0.25
- branch_logit_multiplier: float32 [8], replicated, may hold values from 1 to 30, as said below
Outputs:
- tokens_out: bfloat16 [128, 256, 512], P(('grp', 'rows'), 'cols'), parts along dimension 0
- latent_mix: bfloat16 [512, 512], P('grp'), parts along dimension 0
There are 2 independent parts, one for each index of `grp`. A program takes and returns all parts, laid end to end along the dimension named above; an argument that names none is the same for every part. Nothing has to cross between parts.
Inputs may be any that keep to these rules, and one draw needn't show every extreme that they name: `branch_logit_multiplier`: a positive logit scale for each head.
All inputs are finite; a program needn't handle non-finite values.
Results may differ from a plain program's by a relative error of at most 0.0095.
The roundings to bfloat16 on the way count: a program that leaves them out, or rounds other values in their place, can miss the bound.
Values may be sent and summed in bfloat16 or wider, within the bound.
No kernel may reach another device: no remote copies, remote signals or barrier semaphores. Data moves between devices by JAX's collectives and lax.ppermute only.
A program may use at most 192 MiB of HBM per device.

v0:
```python
import math
import jax
import jax.numpy as jnp
from jax import lax
from jax.sharding import PartitionSpec as P

H = 8
BLK = 8
RIM = 3


def with_halo(array, sides, width):
    for axis, dim in sides:
        devices, length = (lax.axis_size(axis), array.shape[dim])
        up = [(i, (i + 1) % devices) for i in range(devices - 1)]
        down = [(j, i) for i, j in up]
        last = lax.slice_in_dim(array, length - width, length, axis=dim)
        initial = lax.slice_in_dim(array, 0, width, axis=dim)
        before = lax.ppermute(last, axis, up)
        after = lax.ppermute(initial, axis, down)
        array = jnp.concatenate([before, array, after], axis=dim)
    return array


def row_norm(values, gain_vector):
    floats = values.astype(jnp.float32)
    scaled = floats * lax.rsqrt(jnp.mean(floats * floats, axis=-1, keepdims=True) + 1e-05)
    return (scaled * gain_vector).astype(jnp.bfloat16)


def head_norm(floats, head_count):
    shaped = floats.reshape(floats.shape[:-1] + (head_count, floats.shape[-1] // head_count))
    normal = shaped * lax.rsqrt(jnp.mean(shaped * shaped, axis=-1, keepdims=True) + 1e-06)
    return normal.astype(jnp.bfloat16)


def halo_attention(queries, keys_ext, values_ext, inside, logit_divisor):
    rows_all, cols_all, head_count, channels_per_branch = queries.shape
    blocks_across = cols_all // BLK
    window = BLK + 2 * RIM
    offsets = (jnp.arange(blocks_across, dtype=jnp.int32) * BLK)[:, None] + jnp.arange(
        window, dtype=jnp.int32
    )[None, :]

    def one_row(block_row):
        query_blocks = queries.reshape(BLK, blocks_across, BLK, head_count, channels_per_branch)
        query_blocks = query_blocks.transpose(1, 0, 2, 3, 4).reshape(
            blocks_across, BLK * BLK, head_count, channels_per_branch
        )
        key_slab = keys_ext[:, offsets]
        key_blocks = key_slab.transpose(1, 0, 2, 3, 4).reshape(
            blocks_across, window * window, head_count, channels_per_branch
        )
        value_slab = values_ext[:, offsets]
        value_blocks = value_slab.transpose(1, 0, 2, 3, 4).reshape(
            blocks_across, window * window, head_count, channels_per_branch
        )
        mask_slab = inside[:, offsets]
        mask_blocks = mask_slab.transpose(1, 0, 2).reshape(blocks_across, window * window)
        scores = jnp.einsum(
            "bqhd,bkhd->bhqk", query_blocks, key_blocks, preferred_element_type=jnp.float32
        )
        scores = scores * logit_divisor[None, :, None, None]
        scores = jnp.where(mask_blocks[:, None, None, :], scores, -1e30)
        row_peak = jnp.max(scores, axis=-1, keepdims=True)
        expo = jnp.exp(scores - row_peak)
        row_total = jnp.sum(expo, axis=-1)
        weights = expo.astype(jnp.bfloat16)
        output = jnp.einsum(
            "bhqk,bkhd->bqhd", weights, value_blocks, preferred_element_type=jnp.float32
        )
        output = output / row_total.transpose(0, 2, 1)[..., None]
        output = output.reshape(
            blocks_across, BLK, BLK, head_count * channels_per_branch
        ).transpose(1, 0, 2, 3)
        return output.reshape(BLK, cols_all, head_count * channels_per_branch).astype(jnp.bfloat16)

    result = lax.map(one_row, jnp.arange(rows_all // BLK, dtype=jnp.int32))
    return result.reshape(rows_all, cols_all, head_count * channels_per_branch)


def per_device(
    crop_feature_grid,
    pixel_layernorm_gain,
    triple_projection_matrix,
    halo_exit_matrix,
    memory_slots,
    memory_layernorm_gain,
    memory_asking_matrix,
    memory_exit_matrix,
    branch_logit_multiplier,
):
    tile_rows, tile_cols, model_width = crop_feature_grid.shape
    head_count = H
    channels_per_branch = model_width // head_count
    normed = row_norm(crop_feature_grid, pixel_layernorm_gain)
    flat_normed = normed.reshape(-1, model_width)
    logit_divisor = branch_logit_multiplier / math.sqrt(channels_per_branch)
    projected = jnp.dot(flat_normed, triple_projection_matrix, preferred_element_type=jnp.float32)
    projected = projected.reshape(tile_rows, tile_cols, 3 * model_width)
    queries = head_norm(projected[..., :model_width], head_count)
    keys = head_norm(projected[..., model_width : 2 * model_width], head_count)
    values = (
        projected[..., 2 * model_width :]
        .reshape(tile_rows, tile_cols, head_count, channels_per_branch)
        .astype(jnp.bfloat16)
    )
    key_value = jnp.concatenate(
        [
            keys.reshape(tile_rows, tile_cols, model_width),
            values.reshape(tile_rows, tile_cols, model_width),
        ],
        axis=2,
    )
    key_value_ext = with_halo(key_value, (("rows", 0), ("cols", 1)), RIM)
    ext_rows, ext_cols = (key_value_ext.shape[0], key_value_ext.shape[1])
    keys_ext = key_value_ext[..., :model_width].reshape(
        ext_rows, ext_cols, head_count, channels_per_branch
    )
    values_ext = key_value_ext[..., model_width:].reshape(
        ext_rows, ext_cols, head_count, channels_per_branch
    )
    crop_rows = tile_rows * lax.axis_size("rows")
    crop_cols = tile_cols * lax.axis_size("cols")
    row_ids = (
        lax.axis_index("rows") * tile_rows - RIM + jnp.arange(tile_rows + 2 * RIM, dtype=jnp.int32)
    )
    col_ids = (
        lax.axis_index("cols") * tile_cols - RIM + jnp.arange(tile_cols + 2 * RIM, dtype=jnp.int32)
    )
    row_inside = (row_ids >= 0) & (row_ids < crop_rows)
    col_inside = (col_ids >= 0) & (col_ids < crop_cols)
    inside = row_inside[:, None] & col_inside[None, :]
    attended = halo_attention(queries, keys_ext, values_ext, inside, logit_divisor)
    branch = jnp.dot(
        attended.reshape(-1, model_width), halo_exit_matrix, preferred_element_type=jnp.float32
    )
    tokens_out = (
        crop_feature_grid.astype(jnp.float32) + branch.reshape(tile_rows, tile_cols, model_width)
    ).astype(jnp.bfloat16)
    latent_normed = row_norm(memory_slots, memory_layernorm_gain)
    latent_queries = head_norm(
        jnp.dot(latent_normed, memory_asking_matrix, preferred_element_type=jnp.float32), head_count
    )
    keys_heads = keys.reshape(-1, head_count, channels_per_branch).transpose(1, 0, 2)
    values_heads = values.reshape(-1, head_count, channels_per_branch).transpose(1, 0, 2)

    def one_head(operands):
        query_head, key_head, value_head, head_scale = operands
        scores = jnp.dot(query_head, key_head.T, preferred_element_type=jnp.float32) * head_scale
        row_peak = jnp.max(scores, axis=-1)
        expo = jnp.exp(scores - row_peak[:, None])
        row_total = jnp.sum(expo, axis=-1)
        weighted = jnp.dot(
            expo.astype(jnp.bfloat16), value_head, preferred_element_type=jnp.float32
        )
        return (row_peak, row_total, weighted)

    local_peak, local_total, local_sum = lax.map(
        one_head, (latent_queries.transpose(1, 0, 2), keys_heads, values_heads, logit_divisor)
    )
    crop_peak = lax.pmax(local_peak, ("rows", "cols"))
    factor = jnp.exp(local_peak - crop_peak)
    crop_total, crop_sum = lax.psum(
        (local_total * factor, local_sum * factor[..., None]), ("rows", "cols")
    )
    latent_heads = crop_sum / crop_total[..., None]
    latent_attended = latent_heads.transpose(1, 0, 2).reshape(-1, model_width).astype(jnp.bfloat16)
    latent_mix = jnp.dot(
        latent_attended, memory_exit_matrix, preferred_element_type=jnp.float32
    ).astype(jnp.bfloat16)
    return (tokens_out, latent_mix)


def solution(mesh):
    return jax.shard_map(
        per_device,
        mesh=mesh,
        in_specs=(P(("grp", "rows"), "cols", None), P(), P(), P(), P(), P(), P(), P(), P()),
        out_specs=(P(("grp", "rows"), "cols", None), P("grp", None)),
        check_vma=False,
    )
```

profile of v0, /device:TPU:0, one launch (start us, length us, event | category | flops | bytes accessed | tf_op | source)
XLA Modules:
  0.0 278.7 jit_solution(9625256363272125825)
XLA Ops:
  8.9 3.1 %fusion.33 = f32[8,128,1536]{2,1,0:T(8,128)S(1)} fusion(bf16[512,1536]{1,0:T(8,128)(2,1)S(1)} %copy-done, bf16[8,128,512]{2,1,0:T(8,128)(2,1)} %param.11, f32[512]{0:T(512)} %param.12, f32[8,128]{1,0:T(8,128)S(1)} %add_rsqrt_fusion.3), kind=kOutput, calls=%fused_computation.50 | convolution fusion | flops 1612709888 | bytes 8919040 | tf_op jit(solution)/shard_map/dot_general | solution.py:99
  12.0 4.1 %fusion.58 = (f32[8,128,512]{2,1,0:T(8,128)}, f32[8,128,512]{2,1,0:T(8,128)}, f32[8,128,512]{2,1,0:T(8,128)}, f32[8,128,512]{2,1,0:T(8,128)}) fusion(f32[8,128,1536]{2,1,0:T(8,128)S(1)} %fusion.33), kind=kLoop, calls=%fused_computation.97 | loop fusion | flops 1048576 | bytes 12582912 | tf_op jit(solution)/shard_map/slice | solution.py:102
  17.4 2.9 %copy.38 = f32[8,128,512]{1,2,0:T(8,128)} copy(f32[8,128,512]{2,1,0:T(8,128)} %get-tuple-element.110) | data formatting | bytes 4194304 | tf_op jit(solution)/shard_map/mul | solution.py:33
  22.1 2.9 %copy.52 = f32[8,128,512]{1,0,2:T(8,128)} copy(f32[8,128,512]{2,1,0:T(8,128)} %get-tuple-element.109) | data formatting | bytes 4194304 | tf_op jit(solution)/shard_map/slice | solution.py:102
  32.4 32.1 %while.4 = (s32[]{:T(128)}, f32[8,256]{1,0:T(8,128)S(1)}, f32[8,256]{1,0:T(8,128)S(1)}, f32[8,256,64]{1,2,0:T(8,128)}, bf16[8,256,64]{1,2,0:T(8,128)(2,1)S(1)}, ...) while((s32[]{:T(128)}, f32[8,256]{1,0:T(8,128)S(1)}, ...), condition=%wide.region_10.11_spmd, body=%wide.region_7.0_spmd.sunk | while | flops 68681216 | bytes 3517049 | solution.py:159
  64.5 35.4 %pmax.7 = f32[8,256]{1,0:T(8,128)S(1)} all-reduce(f32[8,256]{1,0:T(8,128)S(1)} %get-tuple-element.71), channel_id=1, replica_groups=mesh['grp'=2,'rows'=8,'cols'=2] {'rows','cols'}, use_global_device_ids=true, to_apply=%region_11.12 | all-reduce | flops 2048 | bytes 16384 | tf_op jit(solution)/shard_map/pmax | solution.py:162
  113.1 4.4 %reshape.188 = f32[8,16,8,8,64]{4,3,2,1,0:T(8,128)} reshape(f32[8,128,512]{2,1,0:T(8,128)} %get-tuple-element.112) | data formatting | bytes 4194304 | tf_op jit(solution)/shard_map/reshape | solution.py:32
  117.4 2.9 %copy.43 = f32[8,128,512]{1,2,0:T(8,128)} copy(f32[8,128,512]{2,1,0:T(8,128)} %get-tuple-element.111) | data formatting | bytes 4194304 | tf_op jit(solution)/shard_map/mul | solution.py:33
  124.5 40.9 %psum.15 = f32[8,256]{1,0:T(8,128)S(1)} all-reduce(f32[8,256]{1,0:T(8,128)S(1)} %get-tuple-element.105), channel_id=1, replica_groups=mesh['grp'=2,'rows'=8,'cols'=2] {'rows','cols'}, use_global_device_ids=true, to_apply=%region_13.14 | all-reduce | flops 2048 | bytes 16384 | tf_op jit(solution)/shard_map/psum | solution.py:164
  165.5 3.9 %fusion.30 = bf16[16,8,8,8,64]{4,3,2,0,1:T(8,128)(2,1)} fusion(f32[8,16,8,8,64]{4,3,2,1,0:T(8,128)} %reshape.188, f32[8,16,8,8]{3,2,1,0:T(8,128)} %bitcast.109), kind=kLoop, calls=%fused_computation.42 | loop fusion | flops 1048576 | bytes 3178496 | tf_op jit(solution)/shard_map/while/body/eval_jaxpr/transpose | solution.py:47
  169.4 26.6 %all-reduce.2.cloned.1.call-done = f32[8,256,64]{1,2,0:T(8,128)} async-done(((f32[8,256,64]{1,2,0:T(8,128)}), f32[8,256,64]{1,2,0:T(8,128)}) %all-reduce.2.cloned.1.call-update) | async-done | bytes 524304 | tf_op jit(solution)/shard_map/psum | solution.py:164
  203.7 3.6 %pad_maximum_fusion = bf16[14,134,1024]{2,1,0:T(8,128)(2,1)S(1)} fusion(bf16[14,3,1024]{2,1,0:T(4,128)(2,1)S(1)} %collective-permute-done.3, bf16[3,128,1024]{2,1,0:T(8,128)(2,1)} %collective-permute-done.1, bf16[8,128,512]{2,1,0:T(8,128)(2,1)S(1)} %slice.51, bf16[8,128,512]{2,1,0:T(8,128)(2,1)S(1)} %multiply_convert_fusion.2, ...), kind=kLoop, calls=%fused_computation.34 | loop fusion | flops 23052288 | bytes 7684096 | tf_op jit(solution)/shard_map/concatenate | solution.py:21
  208.9 5.6 %reshape.190 = bf16[14,134,8,64]{3,2,1,0:T(8,128)(2,1)} reshape(bf16[14,134,512]{2,1,0:T(8,128)(2,1)} %get-tuple-element.114) | data formatting | bytes 3842048 | tf_op jit(solution)/shard_map/reshape | solution.py:117
  214.5 7.1 %gather_fusion.2 = bf16[224,14,8,64]{3,2,1,0:T(8,128)(2,1)} fusion(bf16[14,134,8,64]{3,2,1,0:T(8,128)(2,1)} %reshape.190, s32[1024]{0:T(1024)S(1)} %pad_clamp_fusion), kind=kCustom, calls=%fused_computation.2 | custom fusion | bytes 6423424 | tf_op jit(solution)/shard_map/while/body/eval_jaxpr/gather | solution.py:50
  221.5 6.6 %copy.46 = bf16[16,14,14,8,64]{4,3,1,2,0:T(8,128)(2,1)} copy(bf16[16,14,14,8,64]{4,3,2,1,0:T(8,128)(2,1)} %bitcast.104) | data formatting | bytes 6422528 | tf_op jit(solution)/shard_map/while/body/eval_jaxpr/gather | solution.py:50
  228.2 3.3 %reshape.186 = bf16[14,134,8,64]{3,2,1,0:T(8,128)(2,1)} reshape(bf16[14,134,512]{2,1,0:T(8,128)(2,1)S(1)} %get-tuple-element.113) | data formatting | bytes 3842048 | tf_op jit(solution)/shard_map/reshape | solution.py:120
  231.5 7.0 %gather_fusion = bf16[224,14,8,64]{3,2,1,0:T(8,128)(2,1)} fusion(bf16[14,134,8,64]{3,2,1,0:T(8,128)(2,1)} %reshape.186, s32[1024]{0:T(1024)S(1)} %pad_clamp_fusion), kind=kCustom, calls=%fused_computation | custom fusion | bytes 6423424 | tf_op jit(solution)/shard_map/while/body/eval_jaxpr/gather | solution.py:54
  238.5 6.8 %copy.40 = bf16[16,14,14,8,64]{4,3,1,2,0:T(8,128)(2,1)} copy(bf16[16,14,14,8,64]{4,3,2,1,0:T(8,128)(2,1)} %bitcast.103) | data formatting | bytes 6422528 | tf_op jit(solution)/shard_map/while/body/eval_jaxpr/gather | solution.py:54
  245.3 6.5 %fusion.13 = (f32[16,8,64]{2,1,0:T(8,128)S(1)}, f32[16,8,64,196]{3,2,1,0:T(8,128)S(1)}) fusion(f32[8]{0:T(128)S(1)} %get-tuple-element.217, pred[16,196]{1,0:T(8,128)(4,1)S(1)} %broadcast_in_dim.60, bf16[16,196,8,64]{3,2,1,0:T(8,128)(2,1)} %bitcast.106, bf16[16,8,8,8,64]{4,3,2,0,1:T(8,128)(2,1)S(1)} %copy-done.4), kind=kOutput, calls=%fused_computation.20 | convolution fusion | flops 210329600 | bytes 10718304 | tf_op jit(solution)/shard_map/while/body/eval_jaxpr/bqhd,bkhd->bhqk/dot_general | solution.py:60
  251.8 3.7 %fusion.18 = f32[16,8,64]{2,1,0:T(8,128)S(1)} fusion(f32[16,8,64,196]{3,2,1,0:T(8,128)S(1)} %get-tuple-element.122, f32[16,8,64]{2,1,0:T(8,128)S(1)} %get-tuple-element.121, f32[8]{0:T(128)S(1)} %get-tuple-element.217, pred[16,196]{1,0:T(8,128)(4,1)S(1)} %broadcast_in_dim.60), kind=kLoop, calls=%fused_computation.25 | loop fusion | flops 6414336 | bytes 6491232 | tf_op jit(solution)/shard_map/while/body/eval_jaxpr/reduce_sum | solution.py:67
  255.5 6.0 %fusion.21 = bf16[16,64,8,64]{1,3,2,0:T(8,128)(2,1)} fusion(f32[16,64,8]{1,2,0:T(8,128)S(1)} %bitcast.114, f32[16,8,64,196]{3,2,1,0:T(8,128)S(1)} %get-tuple-element.122, f32[16,8,64]{2,1,0:T(8,128)S(1)} %get-tuple-element.121, f32[8]{0:T(128)S(1)} %get-tuple-element.217, pred[16,196]{1,0:T(8,128)(4,1)S(1)} %broadcast_in_dim.60, ...), kind=kOutput, calls=%fused_computation.28 | convolution fusion | flops 212992000 | bytes 10751072 | tf_op jit(solution)/shard_map/while/body/eval_jaxpr/bhqk,bkhd->bqhd/dot_general | solution.py:69
  261.5 4.3 %copy.49 = bf16[16,64,8,64]{3,2,1,0:T(8,128)(2,1)} copy(bf16[16,64,8,64]{1,3,2,0:T(8,128)(2,1)} %fusion.21) | data formatting | bytes 2097152 | tf_op jit(solution)/shard_map/while/body/eval_jaxpr/convert_element_type | solution.py:76
  265.8 3.2 %convert_element_type.79 = bf16[16,8,8,512]{3,2,1,0:T(8,128)(2,1)S(1)} reshape(bf16[16,64,8,64]{3,2,1,0:T(8,128)(2,1)} %copy.49) | data formatting | bytes 2097152 | tf_op jit(solution)/shard_map/while/body/eval_jaxpr/convert_element_type | solution.py:76
  269.0 2.9 %fusion.29 = bf16[8,128,512]{2,1,0:T(8,128)(2,1)} fusion(bf16[8,128,512]{2,1,0:T(8,128)(2,1)} %param.11, bf16[512,512]{1,0:T(8,128)(2,1)S(1)} %copy-done.9, bf16[16,8,8,512]{3,2,1,0:T(8,128)(2,1)S(1)} %convert_element_type.79), kind=kOutput, calls=%fused_computation.41 | convolution fusion | flops 538443776 | bytes 3670016 | tf_op jit(solution)/shard_map/dot_general | solution.py:135
  (123 shorter events, 70.3 us)
Async XLA Ops:
  7.2 1.7 copy-start
  7.2 188.8 %all-reduce.2.cloned.1.call-start = ((), (), s32[]{:S(2)}) async-start(), calls=%async_computation | async-start | bytes 1048576 | tf_op jit(solution)/shard_map/psum | solution.py:164
  12.0 5.2 %copy-start.2 = (f32[8,128,1536]{2,1,0:T(8,128)}, f32[8,128,1536]{2,1,0:T(8,128)S(1)}, u32[]{:S(2)}) copy-start(f32[8,128,1536]{2,1,0:T(8,128)S(1)} %fusion.33) | copy-start | bytes 18874372
  25.1 4.8 %copy-start.10 = (f32[8]{0:T(128)S(1)}, f32[8]{0:T(128)}, u32[]{:S(2)}) copy-start(f32[8]{0:T(128)} %param.19) | copy-start | bytes 100
  25.1 4.8 %copy-start.5 = (bf16[256,512]{1,0:T(8,128)(2,1)S(1)}, bf16[256,512]{1,0:T(8,128)(2,1)}, u32[]{:S(2)}) copy-start(bf16[256,512]{1,0:T(8,128)(2,1)} %param.15) | copy-start | bytes 786436
  25.1 5.0 %copy-start.6 = (bf16[512,512]{1,0:T(8,128)(2,1)S(1)}, bf16[512,512]{1,0:T(8,128)(2,1)}, u32[]{:S(2)}) copy-start(bf16[512,512]{1,0:T(8,128)(2,1)} %param.17) | copy-start | bytes 1572868
  25.1 5.0 %copy-start.8 = (f32[512]{0:T(512)S(1)}, f32[512]{0:T(512)}, u32[]{:S(2)}) copy-start(f32[512]{0:T(512)} %param.16) | copy-start | bytes 6148
  110.2 86.9 %collective-permute-start = (bf16[3,128,1024]{2,1,0:T(8,128)(2,1)}, bf16[3,128,1024]{2,1,0:T(8,128)(2,1)S(1)}, u32[]{:S(2)}, u32[]{:S(2)}) collective-permute-start(bf16[3,128,1024]{2,1,0:T(8,128)(2,1)} %get-tuple-element.117), channel_id=1, source_target_pairs={{0,2},{2,4},{4,6},{6,8},{8,10},{10,12},{12,14},{1,3},{3,5},{5,7},{... | collective-permute-start | bytes 2359304 | tf_op jit(solution)/shard_map/ppermute | solution.py:19
  111.6 85.6 %collective-permute-start.1 = (bf16[3,128,1024]{2,1,0:T(8,128)(2,1)}, bf16[3,128,1024]{2,1,0:T(8,128)(2,1)}, u32[]{:S(2)}, u32[]{:S(2)}) collective-permute-start(bf16[3,128,1024]{2,1,0:T(8,128)(2,1)} %get-tuple-element.118), channel_id=1, source_target_pairs={{2,0},{4,2},{6,4},{8,6},{10,8},{12,10},{14,12},{3,1},{5,3},{7,5},{... | collective-permute-start | bytes 2359304 | tf_op jit(solution)/shard_map/ppermute | solution.py:20
  196.0 6.0 %copy-start.7 = (bf16[512,512]{1,0:T(8,128)(2,1)S(1)}, bf16[512,512]{1,0:T(8,128)(2,1)}, u32[]{:S(2)}) copy-start(bf16[512,512]{1,0:T(8,128)(2,1)} %param.18) | copy-start | bytes 1572868
  198.1 4.9 %collective-permute-start.2 = (bf16[14,3,1024]{2,1,0:T(4,128)(2,1)S(1)}, bf16[14,3,1024]{2,1,0:T(4,128)(2,1)S(1)}, u32[]{:S(2)}, u32[]{:S(2)}) collective-permute-start(bf16[14,3,1024]{2,1,0:T(4,128)(2,1)S(1)} %get-tuple-element.115), channel_id=1, source_target_pairs={{0,1},{2,3},{4,5},{6,7},{8,9},{10,11},{12,13},{14,15},{16,17},{18,... | collective-permute-start | bytes 258056 | tf_op jit(solution)/shard_map/ppermute | solution.py:19
  200.4 3.2 %collective-permute-start.3 = (bf16[14,3,1024]{2,1,0:T(4,128)(2,1)S(1)}, bf16[14,3,1024]{2,1,0:T(4,128)(2,1)S(1)}, u32[]{:S(2)}, u32[]{:S(2)}) collective-permute-start(bf16[14,3,1024]{2,1,0:T(4,128)(2,1)S(1)} %get-tuple-element.116), channel_id=1, source_target_pairs={{1,0},{3,2},{5,4},{7,6},{9,8},{11,10},{13,12},{15,14},{17,16},{19,... | collective-permute-start | bytes 258056 | tf_op jit(solution)/shard_map/ppermute | solution.py:20
  238.5 6.8 %copy-start.4 = (bf16[16,8,8,8,64]{4,3,2,0,1:T(8,128)(2,1)S(1)}, bf16[16,8,8,8,64]{4,3,2,0,1:T(8,128)(2,1)}, u32[]{:S(2)}) copy-start(bf16[16,8,8,8,64]{4,3,2,0,1:T(8,128)(2,1)} %fusion.30) | copy-start | bytes 3145732
  251.8 3.7 %copy-start.3 = (bf16[16,14,14,8,64]{4,3,1,2,0:T(8,128)(2,1)S(1)}, bf16[16,14,14,8,64]{4,3,1,2,0:T(8,128)(2,1)}, u32[]{:S(2)}) copy-start(bf16[16,14,14,8,64]{4,3,1,2,0:T(8,128)(2,1)} %copy.40) | copy-start | bytes 9633796
  261.5 7.5 %copy-start.9 = (bf16[512,512]{1,0:T(8,128)(2,1)S(1)}, bf16[512,512]{1,0:T(8,128)(2,1)}, u32[]{:S(2)}) copy-start(bf16[512,512]{1,0:T(8,128)(2,1)} %param.14) | copy-start | bytes 1572868
  261.5 10.4 %copy-start.1 = (bf16[512,1536]{1,0:T(8,128)(2,1)S(1)}, bf16[512,1536]{1,0:T(8,128)(2,1)}, u32[]{:S(2)}) copy-start(bf16[512,1536]{1,0:T(8,128)(2,1)} %param.13) | copy-start | bytes 4718596
Sparse Core Ops, SparseCore 0:
  102.0 93.8 all-reduce.1
where the time goes:
time: 280 us; the launch traced here: 279 us
  local copies, waits for them, and re-layouts  77.1 us (28%)
  blocking collectives  76.4 us (27%)
  matrix products  43.6 us (16%)
  other arithmetic  33.2 us (12%)
  waiting for transfers between devices  27.3 us (10%)
  between operations  14.4 us (5%)
  starting transfers between devices  6.5 us (2%)
    psum x1, blocking collectives, per_device(): lax.psum((local_total * factor, local_sum * factor[..., None]), ('rows',...  40.9 us
    pmax x1, blocking collectives, per_device(): crop_peak = lax.pmax(local_peak, ('rows', 'cols'))  35.4 us
    psum x1, waiting for transfers between devices, per_device(): lax.psum((local_total * factor, local_sum * factor[..., None]), ('rows',...  26.6 us
    dot_general x8, matrix products, one_head(): jnp.dot(expo.astype(jnp.bfloat16), value_head, preferred_element_type=jnp...  15.1 us
    gather x2, local copies, waits for them, and re-layouts, one_row(): value_slab = values_ext[:, offsets]  13.8 us
    gather x2, local copies, waits for them, and re-layouts, one_row(): key_slab = keys_ext[:, offsets]  13.7 us
    dot_general x8, matrix products, one_head(): jnp.dot(query_head, key_head.T, preferred_element_type=jnp.float32)  8.53 us
    convert_element_type x2, local copies, waits for them, and re-layouts, one_row(): output.reshape(BLK, cols_all, head_count * channels_per_branch)  7.46 us
  transfers between devices with their start and end apart: 5, of which 2 were waited for; matrix products, arithmetic and copies ran while one was open for 9% of the time, Pallas kernels for 0%

commit v1 on v0

--- a/solution.py
+++ b/solution.py
@@ -162,7 +162,7 @@
     crop_peak = lax.pmax(local_peak, ("rows", "cols"))
     factor = jnp.exp(local_peak - crop_peak)
     crop_total, crop_sum = lax.psum(
-        (local_total * factor, local_sum * factor[..., None]), ("rows", "cols")
+        lax.psum((local_total * factor, local_sum * factor[..., None]), "cols"), "rows"
     )
     latent_heads = crop_sum / crop_total[..., None]
     latent_attended = latent_heads.transpose(1, 0, 2).reshape(-1, model_width).astype(jnp.bfloat16)

time: 280 us -> 251 us (0.90)
  blocking collectives: 76.4 us -> 58.7 us
  waiting for transfers between devices: 27.3 us -> 16.8 us
    psum x1 -> x2, waiting for transfers between devices: 26.6 us -> 1.21 us  [the longest x1 1.19 us: per_device(): lax.psum(lax.psum((local_total * factor, local_sum * factor[..., None]),...]
    psum x1 -> x2, blocking collectives: 40.9 us -> 23.2 us  [the longest x1 19.9 us: per_device(): lax.psum(lax.psum((local_total * factor, local_sum * factor[..., None]),...]
    ppermute x2, waiting for transfers between devices: 0.01 us -> 15.5 us  [with_halo(): before = lax.ppermute(last, axis, up)]
  transfers between devices with their start and end apart: 5 -> 6, of which waited for: 2 -> 2; matrix products, arithmetic and copies ran while one was open for 9% -> 37% of each run, Pallas kernels for 0% -> 0%
where the time goes in v1:
time: 251 us; the launch traced here: 249 us
  local copies, waits for them, and re-layouts  76.6 us (31%)
  blocking collectives  58.7 us (23%)
  matrix products  43.8 us (17%)
  other arithmetic  33.1 us (13%)
  waiting for transfers between devices  16.8 us (7%)
  between operations  14.4 us (6%)
  starting transfers between devices  5.73 us (2%)
    pmax x1, blocking collectives, per_device(): crop_peak = lax.pmax(local_peak, ('rows', 'cols'))  35.4 us
    psum x1, blocking collectives, per_device(): lax.psum(lax.psum((local_total * factor, local_sum * factor[..., None]),...  19.9 us
    ppermute x2, waiting for transfers between devices, with_halo(): before = lax.ppermute(last, axis, up)  15.5 us
    dot_general x8, matrix products, one_head(): jnp.dot(expo.astype(jnp.bfloat16), value_head, preferred_element_type=jnp...  15.1 us
    gather x2, local copies, waits for them, and re-layouts, one_row(): value_slab = values_ext[:, offsets]  13.8 us
    gather x2, local copies, waits for them, and re-layouts, one_row(): key_slab = keys_ext[:, offsets]  13.8 us
    dot_general x8, matrix products, one_head(): jnp.dot(query_head, key_head.T, preferred_element_type=jnp.float32)  8.53 us
    convert_element_type x2, local copies, waits for them, and re-layouts, one_row(): output.reshape(BLK, cols_all, head_count * channels_per_branch)  7.5 us
  transfers between devices with their start and end apart: 6, of which 2 were waited for; matrix products, arithmetic and copies ran while one was open for 37% of the time, Pallas kernels for 0%

profile of v1, /device:TPU:0, one launch (start us, length us, event | category | flops | bytes accessed | tf_op | source)
XLA Modules:
  0.0 249.4 jit_solution(1173466186649939139)
XLA Ops:
  8.9 3.1 %fusion.33 = f32[8,128,1536]{2,1,0:T(8,128)S(1)} fusion(bf16[512,1536]{1,0:T(8,128)(2,1)S(1)} %copy-done, bf16[8,128,512]{2,1,0:T(8,128)(2,1)} %param.11, f32[512]{0:T(512)} %param.12, f32[8,128]{1,0:T(8,128)S(1)} %add_rsqrt_fusion.3), kind=kOutput, calls=%fused_computation.50 | convolution fusion | flops 1612709888 | bytes 8919040 | tf_op jit(solution)/shard_map/dot_general | solution.py:99
  12.0 4.1 %fusion.58 = (f32[8,128,512]{2,1,0:T(8,128)}, f32[8,128,512]{2,1,0:T(8,128)}, f32[8,128,512]{2,1,0:T(8,128)}, f32[8,128,512]{2,1,0:T(8,128)}) fusion(f32[8,128,1536]{2,1,0:T(8,128)S(1)} %fusion.33), kind=kLoop, calls=%fused_computation.97 | loop fusion | flops 1048576 | bytes 12582912 | tf_op jit(solution)/shard_map/slice | solution.py:102
  22.3 2.9 %copy.52 = f32[8,128,512]{1,0,2:T(8,128)} copy(f32[8,128,512]{2,1,0:T(8,128)} %get-tuple-element.109) | data formatting | bytes 4194304 | tf_op jit(solution)/shard_map/slice | solution.py:102
  32.5 32.1 %while.4 = (s32[]{:T(128)}, f32[8,256]{1,0:T(8,128)S(1)}, f32[8,256]{1,0:T(8,128)S(1)}, f32[8,256,64]{1,2,0:T(8,128)}, bf16[8,256,64]{1,2,0:T(8,128)(2,1)S(1)}, ...) while((s32[]{:T(128)}, f32[8,256]{1,0:T(8,128)S(1)}, ...), condition=%wide.region_10.11_spmd, body=%wide.region_7.0_spmd.sunk | while | flops 68681216 | bytes 3517049 | solution.py:159
  64.6 35.4 %pmax.7 = f32[8,256]{1,0:T(8,128)S(1)} all-reduce(f32[8,256]{1,0:T(8,128)S(1)} %get-tuple-element.71), channel_id=1, replica_groups=mesh['grp'=2,'rows'=8,'cols'=2] {'rows','cols'}, use_global_device_ids=true, to_apply=%region_11.12 | all-reduce | flops 2048 | bytes 16384 | tf_op jit(solution)/shard_map/pmax | solution.py:162
  113.2 3.0 %copy.43 = f32[8,128,512]{1,2,0:T(8,128)} copy(f32[8,128,512]{2,1,0:T(8,128)} %get-tuple-element.111) | data formatting | bytes 4194304 | tf_op jit(solution)/shard_map/mul | solution.py:33
  118.2 4.4 %reshape.188 = f32[8,16,8,8,64]{4,3,2,1,0:T(8,128)} reshape(f32[8,128,512]{2,1,0:T(8,128)} %get-tuple-element.112) | data formatting | bytes 4194304 | tf_op jit(solution)/shard_map/reshape | solution.py:32
  122.7 3.8 %fusion.30 = bf16[16,8,8,8,64]{4,3,2,0,1:T(8,128)(2,1)} fusion(f32[8,16,8,8,64]{4,3,2,1,0:T(8,128)} %reshape.188, f32[8,16,8,8]{3,2,1,0:T(8,128)S(1)} %bitcast.109), kind=kLoop, calls=%fused_computation.42 | loop fusion | flops 1048576 | bytes 3178496 | tf_op jit(solution)/shard_map/while/body/eval_jaxpr/transpose | solution.py:47
  126.6 15.5 %collective-permute-done = bf16[3,128,1024]{2,1,0:T(8,128)(2,1)S(1)} collective-permute-done((bf16[3,128,1024]{2,1,0:T(8,128)(2,1)}, bf16[3,128,1024]{2,1,0:T(8,128)(2,1)S(1)}, u32[]{:S(2)}, u32[]{:S(2)}) %collective-permute-start) | collective-permute-done | bytes 786464 | tf_op jit(solution)/shard_map/ppermute | solution.py:19
  147.3 3.3 %psum.30 = f32[8,256]{1,0:T(8,128)S(1)} all-reduce(f32[8,256]{1,0:T(8,128)S(1)} %get-tuple-element.105), channel_id=1, replica_groups=mesh['grp'=2,'rows'=8,'cols'=2] {'cols'}, use_global_device_ids=true, to_apply=%region_14.15 | all-reduce | flops 2048 | bytes 16384 | tf_op jit(solution)/shard_map/psum | solution.py:165
  150.6 19.9 %psum.31 = f32[8,256]{1,0:T(8,128)S(1)} all-reduce(f32[8,256]{1,0:T(8,128)S(1)} %psum.30), channel_id=1, replica_groups=mesh['grp'=2,'rows'=8,'cols'=2] {'rows'}, use_global_device_ids=true, to_apply=%region_15.16 | all-reduce | flops 2048 | bytes 16384 | tf_op jit(solution)/shard_map/psum | solution.py:164
  170.6 3.6 %pad_maximum_fusion = bf16[14,134,1024]{2,1,0:T(8,128)(2,1)S(1)} fusion(bf16[14,3,1024]{2,1,0:T(4,128)(2,1)S(1)} %collective-permute-done.3, bf16[3,128,1024]{2,1,0:T(8,128)(2,1)} %collective-permute-done.1, bf16[8,128,512]{2,1,0:T(8,128)(2,1)S(1)} %slice.51, bf16[8,128,512]{2,1,0:T(8,128)(2,1)S(1)} %multiply_convert_fusion.2, ...), kind=kLoop, calls=%fused_computation.34 | loop fusion | flops 23052288 | bytes 7684096 | tf_op jit(solution)/shard_map/concatenate | solution.py:21
  175.8 5.6 %reshape.190 = bf16[14,134,8,64]{3,2,1,0:T(8,128)(2,1)} reshape(bf16[14,134,512]{2,1,0:T(8,128)(2,1)} %get-tuple-element.114) | data formatting | bytes 3842048 | tf_op jit(solution)/shard_map/reshape | solution.py:117
  181.5 7.1 %gather_fusion.2 = bf16[224,14,8,64]{3,2,1,0:T(8,128)(2,1)} fusion(bf16[14,134,8,64]{3,2,1,0:T(8,128)(2,1)} %reshape.190, s32[1024]{0:T(1024)S(1)} %pad_clamp_fusion), kind=kCustom, calls=%fused_computation.2 | custom fusion | bytes 6423424 | tf_op jit(solution)/shard_map/while/body/eval_jaxpr/gather | solution.py:50
  188.6 6.7 %copy.46 = bf16[16,14,14,8,64]{4,3,1,2,0:T(8,128)(2,1)} copy(bf16[16,14,14,8,64]{4,3,2,1,0:T(8,128)(2,1)} %bitcast.104) | data formatting | bytes 6422528 | tf_op jit(solution)/shard_map/while/body/eval_jaxpr/gather | solution.py:50
  195.2 3.3 %reshape.186 = bf16[14,134,8,64]{3,2,1,0:T(8,128)(2,1)} reshape(bf16[14,134,512]{2,1,0:T(8,128)(2,1)S(1)} %get-tuple-element.113) | data formatting | bytes 3842048 | tf_op jit(solution)/shard_map/reshape | solution.py:120
  198.6 7.0 %gather_fusion = bf16[224,14,8,64]{3,2,1,0:T(8,128)(2,1)} fusion(bf16[14,134,8,64]{3,2,1,0:T(8,128)(2,1)} %reshape.186, s32[1024]{0:T(1024)S(1)} %pad_clamp_fusion), kind=kCustom, calls=%fused_computation | custom fusion | bytes 6423424 | tf_op jit(solution)/shard_map/while/body/eval_jaxpr/gather | solution.py:54
  205.6 6.8 %copy.40 = bf16[16,14,14,8,64]{4,3,1,2,0:T(8,128)(2,1)} copy(bf16[16,14,14,8,64]{4,3,2,1,0:T(8,128)(2,1)} %bitcast.103) | data formatting | bytes 6422528 | tf_op jit(solution)/shard_map/while/body/eval_jaxpr/gather | solution.py:54
  212.4 6.5 %fusion.13 = (f32[16,8,64]{2,1,0:T(8,128)S(1)}, f32[16,8,64,196]{3,2,1,0:T(8,128)S(1)}) fusion(f32[8]{0:T(128)S(1)} %get-tuple-element.221, pred[16,196]{1,0:T(8,128)(4,1)S(1)} %broadcast_in_dim.60, bf16[16,196,8,64]{3,2,1,0:T(8,128)(2,1)} %bitcast.106, bf16[16,8,8,8,64]{4,3,2,0,1:T(8,128)(2,1)S(1)} %copy-done.4), kind=kOutput, calls=%fused_computation.20 | convolution fusion | flops 210329600 | bytes 10718304 | tf_op jit(solution)/shard_map/while/body/eval_jaxpr/bqhd,bkhd->bhqk/dot_general | solution.py:60
  218.9 3.7 %fusion.18 = f32[16,8,64]{2,1,0:T(8,128)S(1)} fusion(f32[16,8,64,196]{3,2,1,0:T(8,128)S(1)} %get-tuple-element.122, f32[16,8,64]{2,1,0:T(8,128)S(1)} %get-tuple-element.121, f32[8]{0:T(128)S(1)} %get-tuple-element.221, pred[16,196]{1,0:T(8,128)(4,1)S(1)} %broadcast_in_dim.60), kind=kLoop, calls=%fused_computation.25 | loop fusion | flops 6414336 | bytes 6491232 | tf_op jit(solution)/shard_map/while/body/eval_jaxpr/reduce_sum | solution.py:67
  222.6 6.0 %fusion.21 = bf16[16,64,8,64]{1,3,2,0:T(8,128)(2,1)} fusion(f32[16,64,8]{1,2,0:T(8,128)S(1)} %bitcast.114, f32[16,8,64,196]{3,2,1,0:T(8,128)S(1)} %get-tuple-element.122, f32[16,8,64]{2,1,0:T(8,128)S(1)} %get-tuple-element.121, f32[8]{0:T(128)S(1)} %get-tuple-element.221, pred[16,196]{1,0:T(8,128)(4,1)S(1)} %broadcast_in_dim.60, ...), kind=kOutput, calls=%fused_computation.28 | convolution fusion | flops 212992000 | bytes 10751072 | tf_op jit(solution)/shard_map/while/body/eval_jaxpr/bhqk,bkhd->bqhd/dot_general | solution.py:69
  228.6 4.2 %copy.49 = bf16[16,64,8,64]{3,2,1,0:T(8,128)(2,1)} copy(bf16[16,64,8,64]{1,3,2,0:T(8,128)(2,1)} %fusion.21) | data formatting | bytes 2097152 | tf_op jit(solution)/shard_map/while/body/eval_jaxpr/convert_element_type | solution.py:76
  232.9 3.2 %convert_element_type.79 = bf16[16,8,8,512]{3,2,1,0:T(8,128)(2,1)S(1)} reshape(bf16[16,64,8,64]{3,2,1,0:T(8,128)(2,1)} %copy.49) | data formatting | bytes 2097152 | tf_op jit(solution)/shard_map/while/body/eval_jaxpr/convert_element_type | solution.py:76
  236.1 3.1 %fusion.29 = bf16[8,128,512]{2,1,0:T(8,128)(2,1)} fusion(bf16[8,128,512]{2,1,0:T(8,128)(2,1)} %param.11, bf16[512,512]{1,0:T(8,128)(2,1)} %param.14, bf16[16,8,8,512]{3,2,1,0:T(8,128)(2,1)S(1)} %convert_element_type.79), kind=kOutput, calls=%fused_computation.41 | convolution fusion | flops 538443776 | bytes 3670016 | tf_op jit(solution)/shard_map/dot_general | solution.py:135
  (125 shorter events, 72.3 us)
Async XLA Ops:
  7.2 1.7 copy-start
  7.2 163.4 %all-reduce.3.cloned.1.call-start = ((), (), s32[]{:S(2)}) async-start(), calls=%async_computation | async-start | bytes 1048576 | tf_op jit(solution)/shard_map/psum | solution.py:165
  12.0 5.3 %copy-start.2 = (f32[8,128,1536]{2,1,0:T(8,128)}, f32[8,128,1536]{2,1,0:T(8,128)S(1)}, u32[]{:S(2)}) copy-start(f32[8,128,1536]{2,1,0:T(8,128)S(1)} %fusion.33) | copy-start | bytes 18874372
  25.2 4.8 %copy-start.9 = (f32[8]{0:T(128)S(1)}, f32[8]{0:T(128)}, u32[]{:S(2)}) copy-start(f32[8]{0:T(128)} %param.19) | copy-start | bytes 100
  25.2 4.8 %copy-start.5 = (bf16[256,512]{1,0:T(8,128)(2,1)S(1)}, bf16[256,512]{1,0:T(8,128)(2,1)}, u32[]{:S(2)}) copy-start(bf16[256,512]{1,0:T(8,128)(2,1)} %param.15) | copy-start | bytes 786436
  25.2 5.0 %copy-start.6 = (bf16[512,512]{1,0:T(8,128)(2,1)S(1)}, bf16[512,512]{1,0:T(8,128)(2,1)}, u32[]{:S(2)}) copy-start(bf16[512,512]{1,0:T(8,128)(2,1)} %param.17) | copy-start | bytes 1572868
  25.2 5.0 %copy-start.8 = (f32[512]{0:T(512)S(1)}, f32[512]{0:T(512)}, u32[]{:S(2)}) copy-start(f32[512]{0:T(512)} %param.16) | copy-start | bytes 6148
  102.0 138.4 %all-reduce.5.cloned.1.call-start = ((), (), s32[]{:S(2)}) async-start(), calls=%async_computation.1 | async-start | bytes 1048576 | tf_op jit(solution)/shard_map/psum | solution.py:164
  110.5 31.7 %collective-permute-start = (bf16[3,128,1024]{2,1,0:T(8,128)(2,1)}, bf16[3,128,1024]{2,1,0:T(8,128)(2,1)S(1)}, u32[]{:S(2)}, u32[]{:S(2)}) collective-permute-start(bf16[3,128,1024]{2,1,0:T(8,128)(2,1)} %get-tuple-element.117), channel_id=1, source_target_pairs={{0,2},{2,4},{4,6},{6,8},{8,10},{10,12},{12,14},{1,3},{3,5},{5,7},{... | collective-permute-start | bytes 2359304 | tf_op jit(solution)/shard_map/ppermute | solution.py:19
  111.8 30.4 %collective-permute-start.1 = (bf16[3,128,1024]{2,1,0:T(8,128)(2,1)}, bf16[3,128,1024]{2,1,0:T(8,128)(2,1)}, u32[]{:S(2)}, u32[]{:S(2)}) collective-permute-start(bf16[3,128,1024]{2,1,0:T(8,128)(2,1)} %get-tuple-element.118), channel_id=1, source_target_pairs={{2,0},{4,2},{6,4},{8,6},{10,8},{12,10},{14,12},{3,1},{5,3},{7,5},{... | collective-permute-start | bytes 2359304 | tf_op jit(solution)/shard_map/ppermute | solution.py:20
  143.1 27.5 %collective-permute-start.2 = (bf16[14,3,1024]{2,1,0:T(4,128)(2,1)S(1)}, bf16[14,3,1024]{2,1,0:T(4,128)(2,1)S(1)}, u32[]{:S(2)}, u32[]{:S(2)}) collective-permute-start(bf16[14,3,1024]{2,1,0:T(4,128)(2,1)S(1)} %get-tuple-element.115), channel_id=1, source_target_pairs={{0,1},{2,3},{4,5},{6,7},{8,9},{10,11},{12,13},{14,15},{16,17},{18,... | collective-permute-start | bytes 258056 | tf_op jit(solution)/shard_map/ppermute | solution.py:19
  144.8 25.8 %collective-permute-start.3 = (bf16[14,3,1024]{2,1,0:T(4,128)(2,1)S(1)}, bf16[14,3,1024]{2,1,0:T(4,128)(2,1)S(1)}, u32[]{:S(2)}, u32[]{:S(2)}) collective-permute-start(bf16[14,3,1024]{2,1,0:T(4,128)(2,1)S(1)} %get-tuple-element.116), channel_id=1, source_target_pairs={{1,0},{3,2},{5,4},{7,6},{9,8},{11,10},{13,12},{15,14},{17,16},{19,... | collective-permute-start | bytes 258056 | tf_op jit(solution)/shard_map/ppermute | solution.py:20
  205.6 6.8 %copy-start.4 = (bf16[16,8,8,8,64]{4,3,2,0,1:T(8,128)(2,1)S(1)}, bf16[16,8,8,8,64]{4,3,2,0,1:T(8,128)(2,1)}, u32[]{:S(2)}) copy-start(bf16[16,8,8,8,64]{4,3,2,0,1:T(8,128)(2,1)} %fusion.30) | copy-start | bytes 3145732
  218.9 3.7 %copy-start.3 = (bf16[16,14,14,8,64]{4,3,1,2,0:T(8,128)(2,1)S(1)}, bf16[16,14,14,8,64]{4,3,1,2,0:T(8,128)(2,1)}, u32[]{:S(2)}) copy-start(bf16[16,14,14,8,64]{4,3,1,2,0:T(8,128)(2,1)} %copy.40) | copy-start | bytes 9633796
  228.6 13.9 %copy-start.1 = (bf16[512,1536]{1,0:T(8,128)(2,1)S(1)}, bf16[512,1536]{1,0:T(8,128)(2,1)}, u32[]{:S(2)}) copy-start(bf16[512,1536]{1,0:T(8,128)(2,1)} %param.13) | copy-start | bytes 4718596
  232.9 8.6 %copy-start.7 = (bf16[512,512]{1,0:T(8,128)(2,1)S(1)}, bf16[512,512]{1,0:T(8,128)(2,1)}, u32[]{:S(2)}) copy-start(bf16[512,512]{1,0:T(8,128)(2,1)} %param.18) | copy-start | bytes 1572868
Sparse Core Ops, SparseCore 0:
  102.2 15.9 all-reduce.2
  170.7 69.6 all-reduce.4
